TPU v7x, 32 devices: a whole 2x2x4 slice. The times are simulated.
32 devices in a mesh: parts: 2 (over x), param: 16 (over z, y, core).
Axes of the slice: x: 2, y: 2, z: 4, core: 2. Of those that a mesh axis runs over, the one named last changes fastest.
Arguments:
- inputs: bfloat16 [8192, 4096], P(('parts', 'param')), parts along dimension 0, may hold values from -7 to 7
- out_grads: bfloat16 [8192, 14336], P(('parts', 'param')), parts along dimension 0, may hold values from -7 to 7
- lengths: int32 [32], P(('parts', 'param')), parts along dimension 0, may hold values from 128 to 256, as said below
- example_ids: int32 [32], P(('parts', 'param')), parts along dimension 0, may hold values from 0 to 15, each once
- proj_seeds: int32 [4], P('parts'), parts along dimension 0, may hold values from 1 to 29999
Outputs:
- fisher: float32 [16384, 8192], P(('parts', 'param')), parts along dimension 0
- precond: float32 [32, 8192], P(('parts', 'param')), parts along dimension 0
- kernel: float32 [32, 16], P(('parts', 'param')), parts along dimension 0
There are 2 independent parts, one for each index of `parts`. A program takes and returns all parts, laid end to end along the dimension named above; each array names one. Nothing has to cross between parts.
Inputs may be any that keep to these rules, and one draw needn't show every extreme that they name: `lengths`: each length is a multiple of 128; some example has the full 256 tokens and some has only 128. `example_ids`: a permutation of the group's example indices.
All inputs are finite; a program needn't handle non-finite values.
Results may differ from a plain program's by a relative error of at most 0.007.
The roundings to bfloat16 on the way count: a program that leaves them out, or rounds other values in their place, can miss the bound.
Values may be sent and summed in bfloat16 or wider, within the bound.
A program may use at most 64 MiB of HBM per device.

v0:
```python
import math
import jax
import jax.numpy as jnp
from jax import lax
from jax.sharding import PartitionSpec as P

K_IN = 64
K_OUT = 128
damp_ratio = 0.5


def projection_table(out_dim, fan_in, seed_value):
    row_index = lax.broadcasted_iota(jnp.int32, (fan_in, out_dim), 1)
    col_index = lax.broadcasted_iota(jnp.int32, (fan_in, out_dim), 0)
    hashed = (row_index * 7919 + col_index * 3571 + seed_value * 9973) % 65521
    hashed = hashed * (hashed % 509 + 17) % 65521
    hashed = (hashed * 97 + row_index * 31 + col_index) % 65521
    uniform = hashed.astype(jnp.float32) * (2.0 / 65520.0) - 1.0
    return (uniform * math.sqrt(3.0 / fan_in)).astype(jnp.bfloat16)


def local(inputs, out_grads, lengths, example_ids, proj_seeds):
    highest = lax.Precision.HIGHEST
    ex_dev = lengths.shape[0]
    slot_len = inputs.shape[0] // ex_dev
    table_in = projection_table(K_IN, inputs.shape[1], proj_seeds[0])
    table_out = projection_table(K_OUT, out_grads.shape[1], proj_seeds[1])
    proj_in = jnp.dot(inputs, table_in, preferred_element_type=jnp.float32).astype(jnp.bfloat16)
    proj_out = jnp.dot(out_grads, table_out, preferred_element_type=jnp.float32).astype(
        jnp.bfloat16
    )
    live_rows = (lax.broadcasted_iota(jnp.int32, (ex_dev, slot_len), 1) < lengths[:, None]).reshape(
        ex_dev * slot_len, 1
    )
    proj_in = jnp.where(live_rows, proj_in, jnp.zeros_like(proj_in))
    outer = jnp.einsum(
        "esi,eso->eio",
        proj_in.reshape(ex_dev, slot_len, K_IN),
        proj_out.reshape(ex_dev, slot_len, K_OUT),
        preferred_element_type=jnp.float32,
    )
    gradients = (
        (outer * (1.0 / math.sqrt(slot_len))).reshape(ex_dev, K_IN * K_OUT).astype(jnp.bfloat16)
    )
    gathered, all_ids = (
        lax.all_gather(gradients, "param", axis=0, tiled=True),
        lax.all_gather(example_ids, "param", axis=0, tiled=True),
    )
    example_count = gathered.shape[0]
    proj_width = gathered.shape[1]
    block_rows = proj_width // lax.axis_size("param")
    column_block = lax.dynamic_slice_in_dim(
        gathered, lax.axis_index("param") * block_rows, block_rows, 1
    )
    fisher = (
        lax.dot_general(
            column_block, gathered, (((0,), (0,)), ((), ())), preferred_element_type=jnp.float32
        )
        / example_count
    )
    damping = (
        damp_ratio
        * jnp.sum(jnp.square(gathered.astype(jnp.float32)))
        / (example_count * proj_width)
    )
    gram_matrix = lax.dot_general(
        gathered, gathered, (((1,), (1,)), ((), ())), preferred_element_type=jnp.float32
    )
    system = gram_matrix + damping * example_count * jnp.eye(example_count, dtype=jnp.float32)
    factor = jnp.linalg.cholesky(system)
    solved = jax.scipy.linalg.cho_solve((factor, True), gram_matrix)
    first_slot = lax.axis_index("param") * ex_dev
    own_cols = lax.dynamic_slice_in_dim(solved, first_slot, ex_dev, 1)
    correction = jnp.einsum(
        "jr,jp->rp", own_cols, gathered, precision=highest, preferred_element_type=jnp.float32
    )
    precond = (gradients.astype(jnp.float32) - correction) / damping
    slot_numbers = lax.broadcasted_iota(jnp.int32, (example_count,), 0)
    inverse = jnp.zeros((example_count,), jnp.int32).at[all_ids].set(slot_numbers)
    own_slots = inverse[first_slot + lax.broadcasted_iota(jnp.int32, (ex_dev,), 0)]
    own_grads = jnp.take(gathered, own_slots, axis=0)
    tile_block = lax.dot_general(
        own_grads,
        lax.all_gather(precond.astype(jnp.bfloat16), "param", axis=0, tiled=True),
        (((1,), (1,)), ((), ())),
        preferred_element_type=jnp.float32,
    )
    kernel = (
        jnp.zeros((ex_dev, example_count), jnp.float32).at[:, all_ids].set(tile_block) / proj_width
    )
    return (fisher, precond, kernel)


def solution(mesh):
    placed = (
        P(("parts", "param"), None),
        P(("parts", "param"), None),
        P(("parts", "param")),
        P(("parts", "param")),
        P("parts"),
    )
    return jax.shard_map(
        local,
        mesh=mesh,
        in_specs=placed,
        out_specs=(
            P(("parts", "param"), None),
            P(("parts", "param"), None),
            P(("parts", "param"), None),
        ),
        check_vma=False,
    )
```

profile of v0, /device:TPU:0, one launch (start us, length us, event | category | flops | bytes accessed | tf_op | source)
XLA Modules:
  0.0 117.9 jit_solution(8692307448393772548)
XLA Ops:
  0.6 0.0 copy-start
  2.1 1.2 %dynamic-slice.7 = u32[1]{0:T(128)} dynamic-slice(u32[32]{0:T(128)} %constant.217, u32[]{:T(128)S(6)} %add.156), dynamic_slice_sizes={1} | dynamic-slice | bytes 12
  3.4 0.8 dynamic-update-slice.5
  4.1 13.7 %all-reduce = s32[16]{0:T(128)S(1)} all-reduce(s32[16]{0:T(128)S(1)} %dynamic-update-slice.5), channel_id=1, replica_groups=mesh['parts'=2,'param'=16] {'param'}, use_global_device_ids=true, to_apply=%add | all-reduce | flops 16 | bytes 128
  17.8 0.6 scatter_custom_fusion
  18.5 0.6 dynamic-slice.5
  21.0 1.3 %fusion.127 = (s32[1]{0:T(128)}, s32[1]{0:T(128)}) fusion(s32[2]{0:T(128)} %param.9), kind=kLoop, calls=%fused_computation.144 | loop fusion | bytes 16 | tf_op jit(solution)/shard_map/slice | solution.py:27
  23.7 0.0 copy-done
  23.7 0.0 copy-start.1
  23.7 5.3 %fusion.58 = bf16[64,256]{1,0:T(8,128)(2,1)S(1)} fusion(bf16[256,4096]{1,0:T(8,128)(2,1)S(1)} %copy-done, s32[64]{0:T(128)S(1)} %get-tuple-element.31, s32[]{:T(128)} %bitcast.1, s32[4096]{0:T(1024)S(1)} %iota_multiply_fusion.1, s32[64]{0:T(128)S(1)} %get-tuple-element.32, pred[256]{0:T(512)(128)(4,1)S(1)} %iota_compare_fusion.3), kind=kOutput, calls=%fused_computation.67 | convolution fusion | flops 143687680 | bytes 2147076 | tf_op jit(solution)/shard_map/dot_general | solution.py:28
  29.0 0.0 copy-done.1
  29.1 32.5 %fusion.52.clone.8 = bf16[128,256]{1,0:T(8,128)(2,1)S(1)} fusion(bf16[256,14336]{1,0:T(8,128)(2,1)S(1)} %copy-done.1, s32[128]{0:T(128)S(1)} %get-tuple-element.33, s32[]{:T(128)} %bitcast.2, s32[14336]{0:T(1024)S(1)} %iota_multiply_fusion, s32[128]{0:T(128)S(1)} %get-tuple-element.34), kind=kOutput, calls=%fused_computation.64.clone.clone.clone.clone.clone.clone.clone.1 | convolution fusion | flops 1005617152 | bytes 7463940 | tf_op jit(solution)/shard_map/dot_general | solution.py:29
  61.5 0.1 fusion.62
  61.7 19.4 %all-gather.1 = bf16[16,1,8192]{2,1,0:T(2,128)(2,1)S(1)} all-gather(bf16[1,1,8192]{2,1,0:T(2,128)(2,1)S(1)} %reshape.155), channel_id=1, replica_groups=mesh['parts'=2,'param'=16] {'param'}, dimensions={0}, use_global_device_ids=true | all-gather | bytes 278528 | tf_op jit(solution)/shard_map/all_gather | solution.py:46
  81.1 0.9 multiply_reduce_fusion
  83.3 0.2 fusion.78
  83.5 0.1 copy.12
  83.6 1.5 %cholesky.16 = f32[16,16]{1,0:T(8,128)S(1)} custom-call(f32[16,16]{1,0:T(8,128)S(1)} %fusion.94), custom_call_target="Cholesky" | custom-call | tf_op jit(solution)/shard_map/jit(cholesky)/cholesky | solution.py:70
  85.1 0.6 compare_reduce_fusion
  85.8 0.6 fusion.88
  86.4 1.2 %custom-call.10 = f32[1,16,16]{1,2,0:T(8,128)S(1)} custom-call(f32[1,16,16]{2,1,0:T(8,128)S(1)} %fusion.88), custom_call_target="InvertDiagBlocksLowerTriangular" | custom-call | tf_op jit(solution)/shard_map/jit(_cho_solve)/triangular_solve | solution.py:71
  87.7 0.2 fusion.91
  87.9 0.2 fusion.89
  88.1 0.3 fusion.81
  88.4 0.6 fusion.125
  89.0 19.0 %all-gather = bf16[131072]{0:T(1024)(128)(2,1)S(1)} all-gather(bf16[8192]{0:T(1024)(128)(2,1)S(1)} %get-tuple-element.25), channel_id=2, replica_groups=mesh['parts'=2,'param'=16] {'param'}, dimensions={0}, use_global_device_ids=true | all-gather | bytes 278528 | tf_op jit(solution)/shard_map/all_gather | solution.py:84
  107.9 0.1 reshape.146
  108.1 0.2 convolution_bitcast_fusion
  108.3 0.6 scatter_custom_fusion.1
  108.9 0.5 multiply_bitcast_fusion
  109.4 8.5 %convolution_multiply_fusion = f32[512,8192]{1,0:T(8,128)} fusion(bf16[16,1,8192]{2,0,1:T(8,128)(2,1)S(1)} %get-tuple-element.28, bf16[16,1,512]{2,1,0:T(2,128)(2,1)S(1)} %constant_dynamic-slice_fusion.1), kind=kOutput, calls=%fused_computation.2 | convolution fusion | flops 138412032 | bytes 17055744 | tf_op jit(solution)/shard_map/dot_general | solution.py:56
  (12 shorter events, 0.1 us)
Async XLA Ops:
  0.6 23.0 %copy-start = (bf16[256,4096]{1,0:T(8,128)(2,1)S(1)}, bf16[256,4096]{1,0:T(8,128)(2,1)}, u32[]{:S(2)}) copy-start(bf16[256,4096]{1,0:T(8,128)(2,1)} %param.5) | copy-start | bytes 6291460
  23.7 5.4 %copy-start.1 = (bf16[256,14336]{1,0:T(8,128)(2,1)S(1)}, bf16[256,14336]{1,0:T(8,128)(2,1)}, u32[]{:S(2)}) copy-start(bf16[256,14336]{1,0:T(8,128)(2,1)} %param.6) | copy-start | bytes 22020100
where the time goes:
time: 118 us
  blocking collectives  52.1 us (44%)
  matrix products  47.6 us (40%)
  between operations  6.76 us (6%)
  other arithmetic  6.11 us (5%)
  local copies, waits for them, and re-layouts  5.43 us (5%)
    dot_general x1, matrix products, local(): jnp.dot(out_grads, table_out, preferred_element_type=jnp.float32)  32.5 us
    all_gather x1, blocking collectives, local(): lax.all_gather(gradients, 'param', axis=0, tiled=True)  19.4 us
    all_gather x1, blocking collectives, local(): lax.all_gather(precond.astype(jnp.bfloat16), 'param', axis=0, tiled=True)  19 us
    unnamed x1, blocking collectives  13.7 us
    dot_general x1, matrix products, local(): lax.dot_general(column_block, gathered, (((0,), (0,)), ((), ())), preferr...  8.53 us
    dot_general x1, matrix products, local(): jnp.dot(inputs, table_in, preferred_element_type=jnp.float32)  5.35 us

commit v1 on v0

--- a/solution.py
+++ b/solution.py
@@ -7,6 +7,27 @@
 K_IN = 64
 K_OUT = 128
 damp_ratio = 0.5
+
+
+def gather_around(x, axis, dim):
+    count, index, extent = (lax.axis_size(axis), lax.axis_index(axis), x.shape[dim])
+    right = [(i, (i + 1) % count) for i in range(count)]
+    backward = [(i, (i - 1) % count) for i in range(count)]
+    filled = jnp.zeros((*x.shape[:dim], count * extent, *x.shape[dim + 1 :]), x.dtype)
+    filled = lax.dynamic_update_slice_in_dim(filled, x, index * extent, axis=dim)
+    from_left = from_right = x
+    half = count // 2
+    for step in range(1, half + 1):
+        from_left = lax.ppermute(from_left, axis, right)
+        filled = lax.dynamic_update_slice_in_dim(
+            filled, from_left, (index - step) % count * extent, axis=dim
+        )
+        if step < count - half:
+            from_right = lax.ppermute(from_right, axis, backward)
+            filled = lax.dynamic_update_slice_in_dim(
+                filled, from_right, (index + step) % count * extent, axis=dim
+            )
+    return filled
 
 
 def projection_table(out_dim, fan_in, seed_value):
@@ -81,7 +102,7 @@
     own_grads = jnp.take(gathered, own_slots, axis=0)
     tile_block = lax.dot_general(
         own_grads,
-        lax.all_gather(precond.astype(jnp.bfloat16), "param", axis=0, tiled=True),
+        gather_around(precond.astype(jnp.bfloat16), "param", 0),
         (((1,), (1,)), ((), ())),
         preferred_element_type=jnp.float32,
     )

time: 118 us -> 141 us (1.19)
  starting transfers between devices: 0 us -> 27.2 us
  blocking collectives: 52.1 us -> 36.6 us
  waiting for transfers between devices: 0 us -> 7.98 us
  local copies, waits for them, and re-layouts: 5.43 us -> 12.4 us
  matrix products: 47.6 us -> 43.1 us
    ppermute x0 -> x15, starting transfers between devices: none -> 27.2 us  [the longest x7 26.3 us: gather_around(): from_right = lax.ppermute(from_right, axis, backward)]
    all_gather x1 -> x0, blocking collectives: 19 us -> none  [local(): lax.all_gather(precond.astype(jnp.bfloat16), 'param', axis=0, tiled=True)]
    ppermute x0 -> x15, waiting for transfers between devices: none -> 7.98 us  [the longest x8 7.96 us: gather_around(): from_left = lax.ppermute(from_left, axis, right)]
    dynamic_update_slice x0 -> x16, local copies, waits for them, and re-layouts: none -> 7.6 us  [the longest x8 3.8 us: gather_around(): lax.dynamic_update_slice_in_dim(filled, from_left, (index - step) % count...]
    all_gather x1, blocking collectives: 19.4 us -> 24.6 us  [local(): lax.all_gather(gradients, 'param', axis=0, tiled=True)]
    dot_general x1, matrix products: 32.5 us -> 28 us  [local(): jnp.dot(out_grads, table_out, preferred_element_type=jnp.float32)]
    unnamed x1, blocking collectives: 13.7 us -> 12.1 us
  transfers between devices with their start and end apart: 0 -> 15, of which waited for: 0 -> 5; matrix products, arithmetic and copies ran while one was open for 0% -> 13% of each run, Pallas kernels for 0% -> 0%
where the time goes in v1:
time: 141 us
  matrix products  43.1 us (31%)
  blocking collectives  36.6 us (26%)
  starting transfers between devices  27.2 us (19%)
  local copies, waits for them, and re-layouts  12.4 us (9%)
  waiting for transfers between devices  7.98 us (6%)
  between operations  7.18 us (5%)
  other arithmetic  6.1 us (4%)
    dot_general x1, matrix products, local(): jnp.dot(out_grads, table_out, preferred_element_type=jnp.float32)  28 us
    ppermute x7, starting transfers between devices, gather_around(): from_right = lax.ppermute(from_right, axis, backward)  26.3 us
    all_gather x1, blocking collectives, local(): lax.all_gather(gradients, 'param', axis=0, tiled=True)  24.6 us
    unnamed x1, blocking collectives  12.1 us
    dot_general x1, matrix products, local(): lax.dot_general(column_block, gathered, (((0,), (0,)), ((), ())), preferr...  8.53 us
    ppermute x8, waiting for transfers between devices, gather_around(): from_left = lax.ppermute(from_left, axis, right)  7.96 us
    dot_general x1, matrix products, local(): jnp.dot(inputs, table_in, preferred_element_type=jnp.float32)  5.35 us
    dynamic_update_slice x8, local copies, waits for them, and re-layouts, gather_around(): lax.dynamic_update_slice_in_dim(filled, from_left, (index - step) % count...  3.8 us
  transfers between devices with their start and end apart: 15, of which 5 were waited for; matrix products, arithmetic and copies ran while one was open for 13% of the time, Pallas kernels for 0%

profile of v1, /device:TPU:0, one launch (start us, length us, event | category | flops | bytes accessed | tf_op | source)
XLA Modules:
  0.0 140.6 jit_solution(5934825366307074963)
XLA Ops:
  1.5 1.3 fusion.127
  4.1 28.0 %fusion.52.clone.8 = bf16[128,256]{1,0:T(8,128)(2,1)S(1)} fusion(bf16[256,14336]{1,0:T(8,128)(2,1)} %param.6, s32[128]{0:T(128)S(1)} %get-tuple-element.33, s32[]{:T(128)} %bitcast.2, s32[14336]{0:T(1024)S(1)} %iota_multiply_fusion, s32[128]{0:T(128)S(1)} %get-tuple-element.34), kind=kOutput, calls=%fused_computation.64.clone.clone.clone.clone.clone.clone.clone.1 | convolution fusion | flops 1005617152 | bytes 7463940 | tf_op jit(solution)/shard_map/dot_general | solution.py:50
  32.2 5.3 %fusion.58 = bf16[64,256]{1,0:T(8,128)(2,1)S(1)} fusion(bf16[256,4096]{1,0:T(8,128)(2,1)S(1)} %copy-done, s32[64]{0:T(128)S(1)} %get-tuple-element.31, s32[]{:T(128)} %bitcast.1, s32[4096]{0:T(1024)S(1)} %iota_multiply_fusion.1, s32[64]{0:T(128)S(1)} %get-tuple-element.32, pred[256]{0:T(512)(128)(4,1)S(1)} %iota_compare_fusion.3), kind=kOutput, calls=%fused_computation.67 | convolution fusion | flops 143687680 | bytes 2147076 | tf_op jit(solution)/shard_map/dot_general | solution.py:49
  37.7 24.6 %all-gather = bf16[16,1,8192]{2,1,0:T(2,128)(2,1)S(1)} all-gather(bf16[1,1,8192]{2,1,0:T(2,128)(2,1)S(1)} %reshape.154), channel_id=1, replica_groups=mesh['parts'=2,'param'=16] {'param'}, dimensions={0}, use_global_device_ids=true | all-gather | bytes 278528 | tf_op jit(solution)/shard_map/all_gather | solution.py:67
  62.3 0.9 multiply_reduce_fusion
  64.7 1.5 %cholesky.16 = f32[16,16]{1,0:T(8,128)S(1)} custom-call(f32[16,16]{1,0:T(8,128)S(1)} %fusion.94), custom_call_target="Cholesky" | custom-call | tf_op jit(solution)/shard_map/jit(cholesky)/cholesky | solution.py:91
  66.3 0.6 compare_reduce_fusion
  66.9 0.6 fusion.88
  67.6 1.2 custom-call.10
  69.2 0.3 fusion.81
  69.5 0.6 fusion.125
  70.1 0.4 collective-permute-start
  70.5 4.1 %collective-permute-start.1 = (bf16[1,8192]{1,0:T(2,128)(2,1)S(1)}, bf16[1,8192]{1,0:T(2,128)(2,1)S(1)}, u32[]{:S(2)}, u32[]{:S(2)}) collective-permute-start(bf16[1,8192]{1,0:T(2,128)(2,1)S(1)} %convert_element_type.64), channel_id=1, source_target_pairs={{0,15},{1,0},{2,1},{3,2},{4,3},{5,4},{6,5},{7,6},{8,7},{9,8},{10,9... | collective-permute-start | bytes 49160 | tf_op jit(solution)/shard_map/ppermute | solution.py:26
  74.6 1.6 %collective-permute-done = bf16[1,8192]{1,0:T(2,128)(2,1)S(1)} collective-permute-done((bf16[1,8192]{1,0:T(2,128)(2,1)S(1)}, bf16[1,8192]{1,0:T(2,128)(2,1)S(1)}, u32[]{:S(2)}, u32[]{:S(2)}) %collective-permute-start) | collective-permute-done | bytes 16416 | tf_op jit(solution)/shard_map/ppermute | solution.py:21
  76.2 4.4 %collective-permute-start.3 = (bf16[1,8192]{1,0:T(2,128)(2,1)S(1)}, bf16[1,8192]{1,0:T(2,128)(2,1)S(1)}, u32[]{:S(2)}, u32[]{:S(2)}) collective-permute-start(bf16[1,8192]{1,0:T(2,128)(2,1)S(1)} %collective-permute-done.1), channel_id=1, source_target_pairs={{0,15},{1,0},{2,1},{3,2},{4,3},{5,4},{6,5},{7,6},{8,7},{9,8},{10,9... | collective-permute-start | bytes 49160 | tf_op jit(solution)/shard_map/ppermute | solution.py:26
  80.7 1.6 %collective-permute-done.2 = bf16[1,8192]{1,0:T(2,128)(2,1)S(1)} collective-permute-done((bf16[1,8192]{1,0:T(2,128)(2,1)S(1)}, bf16[1,8192]{1,0:T(2,128)(2,1)S(1)}, u32[]{:S(2)}, u32[]{:S(2)}) %collective-permute-start.2) | collective-permute-done | bytes 16416 | tf_op jit(solution)/shard_map/ppermute | solution.py:21
  82.3 4.4 %collective-permute-start.5 = (bf16[1,8192]{1,0:T(2,128)(2,1)S(1)}, bf16[1,8192]{1,0:T(2,128)(2,1)S(1)}, u32[]{:S(2)}, u32[]{:S(2)}) collective-permute-start(bf16[1,8192]{1,0:T(2,128)(2,1)S(1)} %collective-permute-done.3), channel_id=1, source_target_pairs={{0,15},{1,0},{2,1},{3,2},{4,3},{5,4},{6,5},{7,6},{8,7},{9,8},{10,9... | collective-permute-start | bytes 49160 | tf_op jit(solution)/shard_map/ppermute | solution.py:26
  86.7 1.6 %collective-permute-done.4 = bf16[1,8192]{1,0:T(2,128)(2,1)S(1)} collective-permute-done((bf16[1,8192]{1,0:T(2,128)(2,1)S(1)}, bf16[1,8192]{1,0:T(2,128)(2,1)S(1)}, u32[]{:S(2)}, u32[]{:S(2)}) %collective-permute-start.4) | collective-permute-done | bytes 16416 | tf_op jit(solution)/shard_map/ppermute | solution.py:21
  88.3 4.4 %collective-permute-start.7 = (bf16[1,8192]{1,0:T(2,128)(2,1)S(1)}, bf16[1,8192]{1,0:T(2,128)(2,1)S(1)}, u32[]{:S(2)}, u32[]{:S(2)}) collective-permute-start(bf16[1,8192]{1,0:T(2,128)(2,1)S(1)} %collective-permute-done.5), channel_id=1, source_target_pairs={{0,15},{1,0},{2,1},{3,2},{4,3},{5,4},{6,5},{7,6},{8,7},{9,8},{10,9... | collective-permute-start | bytes 49160 | tf_op jit(solution)/shard_map/ppermute | solution.py:26
  92.7 1.6 %collective-permute-done.6 = bf16[1,8192]{1,0:T(2,128)(2,1)S(1)} collective-permute-done((bf16[1,8192]{1,0:T(2,128)(2,1)S(1)}, bf16[1,8192]{1,0:T(2,128)(2,1)S(1)}, u32[]{:S(2)}, u32[]{:S(2)}) %collective-permute-start.6) | collective-permute-done | bytes 16416 | tf_op jit(solution)/shard_map/ppermute | solution.py:21
  94.3 4.4 %collective-permute-start.9 = (bf16[1,8192]{1,0:T(2,128)(2,1)S(1)}, bf16[1,8192]{1,0:T(2,128)(2,1)S(1)}, u32[]{:S(2)}, u32[]{:S(2)}) collective-permute-start(bf16[1,8192]{1,0:T(2,128)(2,1)S(1)} %collective-permute-done.7), channel_id=1, source_target_pairs={{0,15},{1,0},{2,1},{3,2},{4,3},{5,4},{6,5},{7,6},{8,7},{9,8},{10,9... | collective-permute-start | bytes 49160 | tf_op jit(solution)/shard_map/ppermute | solution.py:26
  98.8 1.6 %collective-permute-done.8 = bf16[1,8192]{1,0:T(2,128)(2,1)S(1)} collective-permute-done((bf16[1,8192]{1,0:T(2,128)(2,1)S(1)}, bf16[1,8192]{1,0:T(2,128)(2,1)S(1)}, u32[]{:S(2)}, u32[]{:S(2)}) %collective-permute-start.8) | collective-permute-done | bytes 16416 | tf_op jit(solution)/shard_map/ppermute | solution.py:21
  101.1 0.6 dynamic-slice.7
  101.7 0.8 dynamic-update-slice.5
  102.4 4.5 %collective-permute-start.11 = (bf16[1,8192]{1,0:T(2,128)(2,1)S(1)}, bf16[1,8192]{1,0:T(2,128)(2,1)S(1)}, u32[]{:S(2)}, u32[]{:S(2)}) collective-permute-start(bf16[1,8192]{1,0:T(2,128)(2,1)S(1)} %collective-permute-done.9), channel_id=1, source_target_pairs={{0,15},{1,0},{2,1},{3,2},{4,3},{5,4},{6,5},{7,6},{8,7},{9,8},{10,9... | collective-permute-start | bytes 49160 | tf_op jit(solution)/shard_map/ppermute | solution.py:26
  106.9 8.5 %convolution_multiply_fusion = f32[512,8192]{1,0:T(8,128)} fusion(bf16[16,1,8192]{2,0,1:T(8,128)(2,1)S(1)} %get-tuple-element.28, bf16[16,1,512]{2,1,0:T(2,128)(2,1)S(1)} %constant_dynamic-slice_fusion.1), kind=kOutput, calls=%fused_computation.2 | convolution fusion | flops 138412032 | bytes 17055744 | tf_op jit(solution)/shard_map/dot_general | solution.py:77
  115.4 12.1 %all-reduce = s32[16]{0:T(128)S(1)} all-reduce(s32[16]{0:T(128)S(1)} %dynamic-update-slice.5), channel_id=1, replica_groups=mesh['parts'=2,'param'=16] {'param'}, use_global_device_ids=true, to_apply=%add | all-reduce | flops 16 | bytes 128
  127.5 0.5 collective-permute-start.14
  128.0 0.6 scatter_custom_fusion
  128.7 0.7 dynamic-slice.5
  131.4 0.5 dynamic_update_slice.48
  132.0 0.5 dynamic_update_slice.49
  132.5 0.5 dynamic_update_slice.50
  133.0 0.5 dynamic_update_slice.51
  133.5 0.5 dynamic_update_slice.52
  133.9 0.5 dynamic_update_slice.53
  134.4 0.5 dynamic_update_slice.54
  134.9 0.5 dynamic_update_slice.55
  135.4 0.5 dynamic_update_slice.56
  135.9 0.5 dynamic_update_slice.57
  136.4 0.5 dynamic_update_slice.58
  136.8 0.5 dynamic_update_slice.59
  137.3 0.5 dynamic_update_slice.60
  137.8 0.5 dynamic_update_slice.61
  138.3 0.5 dynamic_update_slice.62
  138.8 0.5 dynamic_update_slice.63
  139.5 0.6 scatter_custom_fusion.1
  140.1 0.5 multiply_bitcast_fusion
  (41 shorter events, 1.3 us)
Async XLA Ops:
  0.6 31.5 %copy-start = (bf16[256,4096]{1,0:T(8,128)(2,1)S(1)}, bf16[256,4096]{1,0:T(8,128)(2,1)}, u32[]{:S(2)}) copy-start(bf16[256,4096]{1,0:T(8,128)(2,1)} %param.5) | copy-start | bytes 6291460
  37.5 63.6 %copy-start.1 = (u32[32]{0:T(128)S(1)}, u32[32]{0:T(128)}, u32[]{:S(2)}) copy-start(u32[32]{0:T(128)} %constant.315) | copy-start | bytes 388
  70.1 6.1 %collective-permute-start = (bf16[1,8192]{1,0:T(2,128)(2,1)S(1)}, bf16[1,8192]{1,0:T(2,128)(2,1)S(1)}, u32[]{:S(2)}, u32[]{:S(2)}) collective-permute-start(bf16[1,8192]{1,0:T(2,128)(2,1)S(1)} %convert_element_type.64), channel_id=1, source_target_pairs={{0,1},{1,2},{2,3},{3,4},{4,5},{5,6},{6,7},{7,8},{8,9},{9,10},{10,1... | collective-permute-start | bytes 49160 | tf_op jit(solution)/shard_map/ppermute | solution.py:21
  70.5 5.7 %collective-permute-start.1 = (bf16[1,8192]{1,0:T(2,128)(2,1)S(1)}, bf16[1,8192]{1,0:T(2,128)(2,1)S(1)}, u32[]{:S(2)}, u32[]{:S(2)}) collective-permute-start(bf16[1,8192]{1,0:T(2,128)(2,1)S(1)} %convert_element_type.64), channel_id=1, source_target_pairs={{0,15},{1,0},{2,1},{3,2},{4,3},{5,4},{6,5},{7,6},{8,7},{9,8},{10,9... | collective-permute-start | bytes 49160 | tf_op jit(solution)/shard_map/ppermute | solution.py:26
  76.2 6.0 %collective-permute-start.2 = (bf16[1,8192]{1,0:T(2,128)(2,1)S(1)}, bf16[1,8192]{1,0:T(2,128)(2,1)S(1)}, u32[]{:S(2)}, u32[]{:S(2)}) collective-permute-start(bf16[1,8192]{1,0:T(2,128)(2,1)S(1)} %collective-permute-done), channel_id=1, source_target_pairs={{0,1},{1,2},{2,3},{3,4},{4,5},{5,6},{6,7},{7,8},{8,9},{9,10},{10,1... | collective-permute-start | bytes 49160 | tf_op jit(solution)/shard_map/ppermute | solution.py:21
  76.2 6.0 %collective-permute-start.3 = (bf16[1,8192]{1,0:T(2,128)(2,1)S(1)}, bf16[1,8192]{1,0:T(2,128)(2,1)S(1)}, u32[]{:S(2)}, u32[]{:S(2)}) collective-permute-start(bf16[1,8192]{1,0:T(2,128)(2,1)S(1)} %collective-permute-done.1), channel_id=1, source_target_pairs={{0,15},{1,0},{2,1},{3,2},{4,3},{5,4},{6,5},{7,6},{8,7},{9,8},{10,9... | collective-permute-start | bytes 49160 | tf_op jit(solution)/shard_map/ppermute | solution.py:26
  82.3 6.0 %collective-permute-start.4 = (bf16[1,8192]{1,0:T(2,128)(2,1)S(1)}, bf16[1,8192]{1,0:T(2,128)(2,1)S(1)}, u32[]{:S(2)}, u32[]{:S(2)}) collective-permute-start(bf16[1,8192]{1,0:T(2,128)(2,1)S(1)} %collective-permute-done.2), channel_id=1, source_target_pairs={{0,1},{1,2},{2,3},{3,4},{4,5},{5,6},{6,7},{7,8},{8,9},{9,10},{10,1... | collective-permute-start | bytes 49160 | tf_op jit(solution)/shard_map/ppermute | solution.py:21
  82.3 6.0 %collective-permute-start.5 = (bf16[1,8192]{1,0:T(2,128)(2,1)S(1)}, bf16[1,8192]{1,0:T(2,128)(2,1)S(1)}, u32[]{:S(2)}, u32[]{:S(2)}) collective-permute-start(bf16[1,8192]{1,0:T(2,128)(2,1)S(1)} %collective-permute-done.3), channel_id=1, source_target_pairs={{0,15},{1,0},{2,1},{3,2},{4,3},{5,4},{6,5},{7,6},{8,7},{9,8},{10,9... | collective-permute-start | bytes 49160 | tf_op jit(solution)/shard_map/ppermute | solution.py:26
  88.3 6.0 %collective-permute-start.6 = (bf16[1,8192]{1,0:T(2,128)(2,1)S(1)}, bf16[1,8192]{1,0:T(2,128)(2,1)S(1)}, u32[]{:S(2)}, u32[]{:S(2)}) collective-permute-start(bf16[1,8192]{1,0:T(2,128)(2,1)S(1)} %collective-permute-done.4), channel_id=1, source_target_pairs={{0,1},{1,2},{2,3},{3,4},{4,5},{5,6},{6,7},{7,8},{8,9},{9,10},{10,1... | collective-permute-start | bytes 49160 | tf_op jit(solution)/shard_map/ppermute | solution.py:21
  88.3 6.0 %collective-permute-start.7 = (bf16[1,8192]{1,0:T(2,128)(2,1)S(1)}, bf16[1,8192]{1,0:T(2,128)(2,1)S(1)}, u32[]{:S(2)}, u32[]{:S(2)}) collective-permute-start(bf16[1,8192]{1,0:T(2,128)(2,1)S(1)} %collective-permute-done.5), channel_id=1, source_target_pairs={{0,15},{1,0},{2,1},{3,2},{4,3},{5,4},{6,5},{7,6},{8,7},{9,8},{10,9... | collective-permute-start | bytes 49160 | tf_op jit(solution)/shard_map/ppermute | solution.py:26
  94.3 6.0 %collective-permute-start.8 = (bf16[1,8192]{1,0:T(2,128)(2,1)S(1)}, bf16[1,8192]{1,0:T(2,128)(2,1)S(1)}, u32[]{:S(2)}, u32[]{:S(2)}) collective-permute-start(bf16[1,8192]{1,0:T(2,128)(2,1)S(1)} %collective-permute-done.6), channel_id=1, source_target_pairs={{0,1},{1,2},{2,3},{3,4},{4,5},{5,6},{6,7},{7,8},{8,9},{9,10},{10,1... | collective-permute-start | bytes 49160 | tf_op jit(solution)/shard_map/ppermute | solution.py:21
  94.3 8.1 %collective-permute-start.9 = (bf16[1,8192]{1,0:T(2,128)(2,1)S(1)}, bf16[1,8192]{1,0:T(2,128)(2,1)S(1)}, u32[]{:S(2)}, u32[]{:S(2)}) collective-permute-start(bf16[1,8192]{1,0:T(2,128)(2,1)S(1)} %collective-permute-done.7), channel_id=1, source_target_pairs={{0,15},{1,0},{2,1},{3,2},{4,3},{5,4},{6,5},{7,6},{8,7},{9,8},{10,9... | collective-permute-start | bytes 49160 | tf_op jit(solution)/shard_map/ppermute | solution.py:26
  100.4 6.5 %collective-permute-start.10 = (bf16[1,8192]{1,0:T(2,128)(2,1)S(1)}, bf16[1,8192]{1,0:T(2,128)(2,1)S(1)}, u32[]{:S(2)}, u32[]{:S(2)}) collective-permute-start(bf16[1,8192]{1,0:T(2,128)(2,1)S(1)} %collective-permute-done.8), channel_id=1, source_target_pairs={{0,1},{1,2},{2,3},{3,4},{4,5},{5,6},{6,7},{7,8},{8,9},{9,10},{10,1... | collective-permute-start | bytes 49160 | tf_op jit(solution)/shard_map/ppermute | solution.py:21
  102.4 25.1 %collective-permute-start.11 = (bf16[1,8192]{1,0:T(2,128)(2,1)S(1)}, bf16[1,8192]{1,0:T(2,128)(2,1)S(1)}, u32[]{:S(2)}, u32[]{:S(2)}) collective-permute-start(bf16[1,8192]{1,0:T(2,128)(2,1)S(1)} %collective-permute-done.9), channel_id=1, source_target_pairs={{0,15},{1,0},{2,1},{3,2},{4,3},{5,4},{6,5},{7,6},{8,7},{9,8},{10,9... | collective-permute-start | bytes 49160 | tf_op jit(solution)/shard_map/ppermute | solution.py:26
  106.9 20.6 %collective-permute-start.12 = (bf16[1,8192]{1,0:T(2,128)(2,1)S(1)}, bf16[1,8192]{1,0:T(2,128)(2,1)S(1)}, u32[]{:S(2)}, u32[]{:S(2)}) collective-permute-start(bf16[1,8192]{1,0:T(2,128)(2,1)S(1)} %collective-permute-done.10), channel_id=1, source_target_pairs={{0,1},{1,2},{2,3},{3,4},{4,5},{5,6},{6,7},{7,8},{8,9},{9,10},{10,1... | collective-permute-start | bytes 49160 | tf_op jit(solution)/shard_map/ppermute | solution.py:21
  127.5 10.8 %collective-permute-start.13 = (bf16[1,8192]{1,0:T(2,128)(2,1)S(1)}, bf16[1,8192]{1,0:T(2,128)(2,1)S(1)}, u32[]{:S(2)}, u32[]{:S(2)}) collective-permute-start(bf16[1,8192]{1,0:T(2,128)(2,1)S(1)} %collective-permute-done.11), channel_id=1, source_target_pairs={{0,15},{1,0},{2,1},{3,2},{4,3},{5,4},{6,5},{7,6},{8,7},{9,8},{10,9... | collective-permute-start | bytes 49160 | tf_op jit(solution)/shard_map/ppermute | solution.py:26
  127.5 11.3 %collective-permute-start.14 = (bf16[1,8192]{1,0:T(2,128)(2,1)S(1)}, bf16[1,8192]{1,0:T(2,128)(2,1)S(1)}, u32[]{:S(2)}, u32[]{:S(2)}) collective-permute-start(bf16[1,8192]{1,0:T(2,128)(2,1)S(1)} %collective-permute-done.12), channel_id=1, source_target_pairs={{0,1},{1,2},{2,3},{3,4},{4,5},{5,6},{6,7},{7,8},{8,9},{9,10},{10,1... | collective-permute-start | bytes 49160 | tf_op jit(solution)/shard_map/ppermute | solution.py:21
